TPU v7x, 32 devices: a whole 2x2x4 slice. The times are simulated.
32 devices in a mesh: gas: 8 (over z, y), space: 4 (over x, core).
Axes of the slice: x: 2, y: 2, z: 4, core: 2. Of those that a mesh axis runs over, the one named last changes fastest.
Arguments:
- particle_amount: bfloat16 [1024, 256, 8, 128], P('gas', 'space'), may hold values from 0 to 1
- section_opacity: bfloat16 [1024, 16], P('gas'), may hold values from 0.0009994507 to 0.0099487305
- species_opacity_factor: float32 [16], replicated, may hold values from 0.05 to 0.5
- absorber_molefraction: float32 [256, 8, 128], P('space'), may hold values from 0 to 1
- scaled_heat_level: float32 [256, 8, 128], P('space'), may hold values from 0.24 to 1.68
- wall_touching_flag: int32 [256, 8, 128], P('space'), may hold values 0 or 1
- fraction_polynomial: float32 [16, 3], replicated, may hold values from 0.05 to 1.35
Outputs:
- divergence: float32 [256, 8, 128], P('space')
- average_radiative_loss: float32 [], replicated
All inputs are finite; a program needn't handle non-finite values. No bound on the sum of `wall_touching_flag` on one device may be relied on, other than what follows from the above.
Results may differ from a plain program's by a relative error of at most 0.0003.
Values sent between devices are 32-bit elements; how exact they have to be, the bound alone decides.
A program may use at most 64 MiB of HBM per device.

v0:
```python
import jax
import jax.numpy as jnp
from jax import lax
from jax.sharding import PartitionSpec as P

SWEEPS = 6
KAPPA_FLOOR = 0.5
WALL_LOSS = 0.5
LAM_LOW = 0.5
LAM_HIGH = 12.0


def with_halo(x, sides, width):
    for axis, dim in sides:
        peers, length = (lax.axis_size(axis), x.shape[dim])
        up = [(i, (i + 1) % peers) for i in range(peers - 1)]
        down = [(j, i) for i, j in up]
        last = lax.slice_in_dim(x, length - width, length, axis=dim)
        leading = lax.slice_in_dim(x, 0, width, axis=dim)
        before = lax.ppermute(last, axis, up)
        after = lax.ppermute(leading, axis, down)
        x = jnp.concatenate([before, x, after], axis=dim)
    return x


def lower(values, dimension):
    border = jnp.zeros_like(lax.slice_in_dim(values, 0, 1, axis=dimension))
    return jnp.concatenate(
        [border, lax.slice_in_dim(values, 0, values.shape[dimension] - 1, axis=dimension)],
        dimension,
    )


def upper(values, dimension):
    border = jnp.zeros_like(lax.slice_in_dim(values, 0, 1, axis=dimension))
    return jnp.concatenate(
        [lax.slice_in_dim(values, 1, values.shape[dimension], axis=dimension), border], dimension
    )


def coupling(paired_total):
    positive = paired_total > 0.0
    return jnp.where(positive, 2.0 / (3.0 * jnp.where(positive, paired_total, 1.0)), 0.0)


def per_device(
    particle_amount,
    section_opacity,
    species_opacity_factor,
    absorber_molefraction,
    scaled_heat_level,
    wall_touching_flag,
    fraction_polynomial,
):
    gas_count = lax.axis_size("gas")
    per_gas = species_opacity_factor.shape[0] // gas_count
    first_gas = lax.axis_index("gas") * per_gas
    width_x = absorber_molefraction.shape[0]
    total_x = width_x * lax.axis_size("space")
    soot_flat = particle_amount.reshape(particle_amount.shape[0], -1)
    summed_all = lax.psum(
        lax.dot_general(
            section_opacity, soot_flat, (((0,), (0,)), ((), ())), preferred_element_type=jnp.float32
        ),
        "gas",
    )
    own_soot = lax.dynamic_slice_in_dim(summed_all, first_gas, per_gas, 0)
    own_soot = own_soot.reshape((per_gas,) + absorber_molefraction.shape)
    strength = lax.dynamic_slice_in_dim(species_opacity_factor, first_gas, per_gas, 0)
    component_lines = lax.dynamic_slice_in_dim(fraction_polynomial, first_gas, per_gas, 0)
    absorption = (
        KAPPA_FLOOR + strength[:, None, None, None] * absorber_molefraction[None] + own_soot
    )
    heat_level_square = scaled_heat_level * scaled_heat_level
    component_fractions = (
        component_lines[:, 0][:, None, None, None]
        + component_lines[:, 1][:, None, None, None] * scaled_heat_level[None]
        + component_lines[:, 2][:, None, None, None] * heat_level_square[None]
    )
    emitted_power = component_fractions * (heat_level_square * heat_level_square)[None]
    base_diag = absorption + WALL_LOSS * wall_touching_flag.astype(jnp.float32)[None]
    halo_depth = 1
    widened = with_halo(jnp.stack([absorption, base_diag]), (("space", 2),), halo_depth)
    wide_abs = widened[0]
    inner_abs = wide_abs[:, 1:-1]
    couple = (
        coupling(inner_abs + wide_abs[:, :-2]),
        coupling(inner_abs + wide_abs[:, 2:]),
        coupling(inner_abs + lower(inner_abs, 2)),
        coupling(inner_abs + upper(inner_abs, 2)),
        coupling(inner_abs + lower(inner_abs, 3)),
        coupling(inner_abs + upper(inner_abs, 3)),
    )
    diagonal = widened[1][:, 1:-1]
    for weight_face in couple:
        diagonal = diagonal + weight_face
    rows_wide = width_x + 2 * halo_depth - 2
    global_row = (
        lax.axis_index("space") * width_x - halo_depth + 1 + jnp.arange(rows_wide, dtype=jnp.int32)
    )
    inside = ((global_row >= 0) & (global_row < total_x)).astype(jnp.float32)[None, :, None, None]
    centre = (LAM_HIGH + LAM_LOW) / 2.0
    spread_half = (LAM_HIGH - LAM_LOW) / 2.0
    ratio_sigma = centre / spread_half
    residual = absorption * emitted_power
    direction = residual / centre
    iterate = jnp.zeros_like(residual)
    ratio_now = 1.0 / ratio_sigma
    for sweep_index in range(SWEEPS):
        residual, direction = (residual, with_halo(direction, (("space", 1),), 1))
        span_rows = direction.shape[1]
        middle = direction[:, 1:-1]
        applied = diagonal * middle
        beside = (
            direction[:, :-2],
            direction[:, 2:],
            lower(middle, 2),
            upper(middle, 2),
            lower(middle, 3),
            upper(middle, 3),
        )
        for weight_face, neighbour in zip(couple, beside):
            applied = applied - weight_face * neighbour
        inner_start = (span_rows - width_x) // 2
        iterate = iterate + direction[:, inner_start : inner_start + width_x]
        residual = (residual - applied) * inside
        ratio_next = 1.0 / (2.0 * ratio_sigma - ratio_now)
        direction = (
            ratio_next * ratio_now * middle + 2.0 * ratio_next / spread_half * residual
        ) * inside
        ratio_now = ratio_next
    gas_terms = absorption * (emitted_power - iterate)
    divergence = lax.psum(jnp.sum(gas_terms, axis=0), "gas")
    cell_count = total_x * absorber_molefraction.shape[1] * absorber_molefraction.shape[2]
    average_radiative_loss = lax.psum(jnp.sum(divergence), "space") / cell_count
    return (divergence, average_radiative_loss)


def solution(mesh):
    return jax.shard_map(
        per_device,
        mesh=mesh,
        in_specs=(
            P("gas", "space", None, None),
            P("gas", None),
            P(),
            P("space", None, None),
            P("space", None, None),
            P("space", None, None),
            P(),
        ),
        out_specs=(P("space", None, None), P()),
        check_vma=False,
    )
```

profile of v0, /device:TPU:0, one launch (start us, length us, event | category | flops | bytes accessed | tf_op | source)
XLA Modules:
  0.0 324.8 jit_solution(6322552649570124776)
XLA Ops:
  7.9 16.8 %fusion = f32[16,65536]{1,0:T(8,128)} fusion(bf16[128,16]{0,1:T(8,128)(2,1)S(1)} %copy-done, bf16[16,8,512,128]{3,2,1,0:T(8,128)(2,1)} %bitcast.31), kind=kOutput, calls=%fused_computation | convolution fusion | flops 268435456 | bytes 20975616 | tf_op jit(solution)/shard_map/dot_general | solution.py:62
  25.7 158.1 %all-reduce.27.cloned.1.call-done = f32[16,65536]{1,0:T(8,128)} async-done(((f32[16,65536]{1,0:T(8,128)}), f32[16,65536]{1,0:T(8,128)}) %all-reduce.27.cloned.1.call-update) | async-done | bytes 4194320 | tf_op jit(solution)/shard_map/psum | solution.py:61
  183.8 1.8 dynamic-slice_bitcast_fusion
  186.3 1.7 collective-permute-start
  188.0 1.3 collective-permute-start.1
  189.3 4.3 %collective-permute-start.2 = (f32[2,1,8,128]{3,2,1,0:T(8,128)S(1)}, f32[2,1,8,128]{3,2,1,0:T(8,128)S(1)}, u32[]{:S(2)}, u32[]{:S(2)}) collective-permute-start(f32[2,1,8,128]{3,2,1,0:T(8,128)S(1)} %get-tuple-element.47), channel_id=1, source_target_pairs={{0,1},{1,2},{2,3},{4,5},{5,6},{6,7},{8,9},{9,10},{10,11},{12,13},{... | collective-permute-start | bytes 24584 | tf_op jit(solution)/shard_map/ppermute | solution.py:20
  193.7 1.5 collective-permute-start.3
  195.6 2.4 collective-permute-done.3
  198.0 1.6 add_multiply_fusion.3
  199.8 4.3 %collective-permute-start.4 = (f32[2,1,8,128]{3,2,1,0:T(8,128)S(1)}, f32[2,1,8,128]{3,2,1,0:T(8,128)S(1)}, u32[]{:S(2)}, u32[]{:S(2)}) collective-permute-start(f32[2,1,8,128]{3,2,1,0:T(8,128)S(1)} %get-tuple-element.41), channel_id=1, source_target_pairs={{0,1},{1,2},{2,3},{4,5},{5,6},{6,7},{8,9},{9,10},{10,11},{12,13},{... | collective-permute-start | bytes 24584 | tf_op jit(solution)/shard_map/ppermute | solution.py:20
  205.5 1.7 collective-permute-done.5
  208.0 3.8 %collective-permute-start.6 = (f32[2,1,8,128]{3,2,1,0:T(8,128)S(1)}, f32[2,1,8,128]{3,2,1,0:T(8,128)S(1)}, u32[]{:S(2)}, u32[]{:S(2)}) collective-permute-start(f32[2,1,8,128]{3,2,1,0:T(8,128)S(1)} %get-tuple-element.35), channel_id=1, source_target_pairs={{0,1},{1,2},{2,3},{4,5},{5,6},{6,7},{8,9},{9,10},{10,11},{12,13},{... | collective-permute-start | bytes 24584 | tf_op jit(solution)/shard_map/ppermute | solution.py:20
  213.2 1.7 collective-permute-done.7
  216.2 3.8 %collective-permute-start.8 = (f32[2,1,8,128]{3,2,1,0:T(8,128)S(1)}, f32[2,1,8,128]{3,2,1,0:T(8,128)S(1)}, u32[]{:S(2)}, u32[]{:S(2)}) collective-permute-start(f32[2,1,8,128]{3,2,1,0:T(8,128)S(1)} %get-tuple-element.29), channel_id=1, source_target_pairs={{0,1},{1,2},{2,3},{4,5},{5,6},{6,7},{8,9},{9,10},{10,11},{12,13},{... | collective-permute-start | bytes 24584 | tf_op jit(solution)/shard_map/ppermute | solution.py:20
  220.0 1.3 collective-permute-start.9
  221.4 1.7 collective-permute-done.9
  223.1 2.1 add_multiply_fusion
  225.4 3.8 %collective-permute-start.10 = (f32[2,1,8,128]{3,2,1,0:T(8,128)S(1)}, f32[2,1,8,128]{3,2,1,0:T(8,128)S(1)}, u32[]{:S(2)}, u32[]{:S(2)}) collective-permute-start(f32[2,1,8,128]{3,2,1,0:T(8,128)S(1)} %get-tuple-element.23), channel_id=1, source_target_pairs={{0,1},{1,2},{2,3},{4,5},{5,6},{6,7},{8,9},{9,10},{10,11},{12,13},{... | collective-permute-start | bytes 24584 | tf_op jit(solution)/shard_map/ppermute | solution.py:20
  230.6 1.7 collective-permute-done.11
  232.3 3.9 %fusion.77 = f32[64,8,128]{2,1,0:T(8,128)} fusion(f32[2,64,8,128]{3,2,1,0:T(8,128)S(1)} %get-tuple-element.10, f32[2,64,8,127]{3,2,1,0:T(8,128)S(1)} %get-tuple-element.28, f32[2,64,8,128]{3,2,1,0:T(8,128)S(1)} %get-tuple-element.7, f32[2,64,8,127]{3,2,1,0:T(8,128)S(1)} %get-tuple-element.27, f32[2,64,8,128]{3,2,1,0:T(8,128)S(1)} %get-tuple-element.6, ...), kind=kLoop, calls=%fused_computation.113 | loop fusion | flops 13172736 | bytes 16548128 | tf_op jit(solution)/shard_map/reduce_sum | solution.py:133
  236.2 70.4 %all-reduce.29.cloned.1.call-done = f32[64,8,128]{2,1,0:T(8,128)} async-done(((f32[64,8,128]{2,1,0:T(8,128)}), f32[64,8,128]{2,1,0:T(8,128)}) %all-reduce.29.cloned.1.call-update) | async-done | bytes 262160 | tf_op jit(solution)/shard_map/psum | solution.py:133
  306.6 1.6 reduce_sum.19
  308.2 6.3 %psum.23 = f32[]{:T(128)} all-reduce(f32[]{:T(128)} %reduce_sum.19), channel_id=1, replica_groups=mesh['gas'=8,'space'=4] {'space'}, use_global_device_ids=true, to_apply=%region_4.5 | all-reduce | flops 1 | bytes 8 | tf_op jit(solution)/shard_map/psum | solution.py:135
  315.2 1.7 copy.26
  (56 shorter events, 9.5 us)
Async XLA Ops:
  7.2 0.7 copy-start
  7.2 176.6 %all-reduce.27.cloned.1.call-start = ((), (), s32[]{:S(2)}) async-start(), calls=%async_computation | async-start | bytes 8388608 | tf_op jit(solution)/shard_map/psum | solution.py:61
  24.6 0.7 copy-start.5
  24.6 0.7 copy-start.4
  24.6 1.0 copy-start.3
  24.6 1.1 copy-start.1
  24.6 160.9 %copy-start.2 = (f32[64,8,128]{2,1,0:T(8,128)S(1)}, f32[64,8,128]{2,1,0:T(8,128)}, u32[]{:S(2)}) copy-start(f32[64,8,128]{2,1,0:T(8,128)} %param.10) | copy-start | bytes 786436
  24.7 281.9 %all-reduce.29.cloned.1.call-start = ((), (), s32[]{:S(2)}) async-start(), calls=%async_computation.1 | async-start | bytes 524288 | tf_op jit(solution)/shard_map/psum | solution.py:133
  186.3 8.8 %collective-permute-start = (f32[2,2,1,8,128]{4,3,2,1,0:T(8,128)S(1)}, f32[2,2,1,8,128]{4,3,2,1,0:T(8,128)S(1)}, u32[]{:S(2)}, u32[]{:S(2)}) collective-permute-start(f32[2,2,1,8,128]{4,3,2,1,0:T(8,128)S(1)} %get-tuple-element.17), channel_id=1, source_target_pairs={{0,1},{1,2},{2,3},{4,5},{5,6},{6,7},{8,9},{9,10},{10,11},{12,13},{... | collective-permute-start | bytes 49160 | tf_op jit(solution)/shard_map/ppermute | solution.py:20
  188.0 7.1 %collective-permute-start.1 = (f32[2,2,1,8,128]{4,3,2,1,0:T(8,128)S(1)}, f32[2,2,1,8,128]{4,3,2,1,0:T(8,128)S(1)}, u32[]{:S(2)}, u32[]{:S(2)}) collective-permute-start(f32[2,2,1,8,128]{4,3,2,1,0:T(8,128)S(1)} %get-tuple-element.18), channel_id=1, source_target_pairs={{1,0},{2,1},{3,2},{5,4},{6,5},{7,6},{9,8},{10,9},{11,10},{13,12},{... | collective-permute-start | bytes 49160 | tf_op jit(solution)/shard_map/ppermute | solution.py:21
  189.3 6.3 %collective-permute-start.2 = (f32[2,1,8,128]{3,2,1,0:T(8,128)S(1)}, f32[2,1,8,128]{3,2,1,0:T(8,128)S(1)}, u32[]{:S(2)}, u32[]{:S(2)}) collective-permute-start(f32[2,1,8,128]{3,2,1,0:T(8,128)S(1)} %get-tuple-element.47), channel_id=1, source_target_pairs={{0,1},{1,2},{2,3},{4,5},{5,6},{6,7},{8,9},{9,10},{10,11},{12,13},{... | collective-permute-start | bytes 24584 | tf_op jit(solution)/shard_map/ppermute | solution.py:20
  193.7 4.3 %collective-permute-start.3 = (f32[2,1,8,128]{3,2,1,0:T(8,128)S(1)}, f32[2,1,8,128]{3,2,1,0:T(8,128)S(1)}, u32[]{:S(2)}, u32[]{:S(2)}) collective-permute-start(f32[2,1,8,128]{3,2,1,0:T(8,128)S(1)} %get-tuple-element.48), channel_id=1, source_target_pairs={{1,0},{2,1},{3,2},{5,4},{6,5},{7,6},{9,8},{10,9},{11,10},{13,12},{... | collective-permute-start | bytes 24584 | tf_op jit(solution)/shard_map/ppermute | solution.py:21
  199.8 5.7 %collective-permute-start.4 = (f32[2,1,8,128]{3,2,1,0:T(8,128)S(1)}, f32[2,1,8,128]{3,2,1,0:T(8,128)S(1)}, u32[]{:S(2)}, u32[]{:S(2)}) collective-permute-start(f32[2,1,8,128]{3,2,1,0:T(8,128)S(1)} %get-tuple-element.41), channel_id=1, source_target_pairs={{0,1},{1,2},{2,3},{4,5},{5,6},{6,7},{8,9},{9,10},{10,11},{12,13},{... | collective-permute-start | bytes 24584 | tf_op jit(solution)/shard_map/ppermute | solution.py:20
  204.1 3.1 collective-permute-start.5
  208.0 5.2 %collective-permute-start.6 = (f32[2,1,8,128]{3,2,1,0:T(8,128)S(1)}, f32[2,1,8,128]{3,2,1,0:T(8,128)S(1)}, u32[]{:S(2)}, u32[]{:S(2)}) collective-permute-start(f32[2,1,8,128]{3,2,1,0:T(8,128)S(1)} %get-tuple-element.35), channel_id=1, source_target_pairs={{0,1},{1,2},{2,3},{4,5},{5,6},{6,7},{8,9},{9,10},{10,11},{12,13},{... | collective-permute-start | bytes 24584 | tf_op jit(solution)/shard_map/ppermute | solution.py:20
  211.8 3.1 collective-permute-start.7
  216.2 5.2 %collective-permute-start.8 = (f32[2,1,8,128]{3,2,1,0:T(8,128)S(1)}, f32[2,1,8,128]{3,2,1,0:T(8,128)S(1)}, u32[]{:S(2)}, u32[]{:S(2)}) collective-permute-start(f32[2,1,8,128]{3,2,1,0:T(8,128)S(1)} %get-tuple-element.29), channel_id=1, source_target_pairs={{0,1},{1,2},{2,3},{4,5},{5,6},{6,7},{8,9},{9,10},{10,11},{12,13},{... | collective-permute-start | bytes 24584 | tf_op jit(solution)/shard_map/ppermute | solution.py:20
  220.0 3.1 collective-permute-start.9
  225.4 5.2 %collective-permute-start.10 = (f32[2,1,8,128]{3,2,1,0:T(8,128)S(1)}, f32[2,1,8,128]{3,2,1,0:T(8,128)S(1)}, u32[]{:S(2)}, u32[]{:S(2)}) collective-permute-start(f32[2,1,8,128]{3,2,1,0:T(8,128)S(1)} %get-tuple-element.23), channel_id=1, source_target_pairs={{0,1},{1,2},{2,3},{4,5},{5,6},{6,7},{8,9},{9,10},{10,11},{12,13},{... | collective-permute-start | bytes 24584 | tf_op jit(solution)/shard_map/ppermute | solution.py:20
  229.2 3.1 collective-permute-start.11
Sparse Core Ops, SparseCore 0:
  24.8 158.9 all-reduce.26
  236.3 70.2 all-reduce.28
where the time goes:
time: 325 us
  waiting for transfers between devices  238 us (73%)
  starting transfers between devices  29.9 us (9%)
  matrix products  16.8 us (5%)
  between operations  16.2 us (5%)
  other arithmetic  11.4 us (4%)
  local copies, waits for them, and re-layouts  6.74 us (2%)
  blocking collectives  6.27 us (2%)
    psum x1, waiting for transfers between devices, per_device(): lax.psum(lax.dot_general(section_opacity, soot_flat, (((0,), (0,)), ((),...  158 us
    psum x1, waiting for transfers between devices, per_device(): divergence = lax.psum(jnp.sum(gas_terms, axis=0), 'gas')  70.4 us
    ppermute x6, starting transfers between devices, with_halo(): before = lax.ppermute(last, axis, up)  21.9 us
    dot_general x1, matrix products, per_device(): lax.dot_general(section_opacity, soot_flat, (((0,), (0,)), ((), ())), pre...  16.8 us
    ppermute x6, waiting for transfers between devices, with_halo(): after = lax.ppermute(leading, axis, down)  9.07 us
    ppermute x6, starting transfers between devices, with_halo(): after = lax.ppermute(leading, axis, down)  7.93 us
  transfers between devices with their start and end apart: 14, of which 7 were waited for; matrix products, arithmetic and copies ran while one was open for 0% of the time, Pallas kernels for 0%

commit v1 on v0

--- a/solution.py
+++ b/solution.py
@@ -58,12 +58,11 @@
     width_x = absorber_molefraction.shape[0]
     total_x = width_x * lax.axis_size("space")
     soot_flat = particle_amount.reshape(particle_amount.shape[0], -1)
-    summed_all = lax.psum(
-        lax.dot_general(
-            section_opacity, soot_flat, (((0,), (0,)), ((), ())), preferred_element_type=jnp.float32
-        ),
-        "gas",
+    value = lax.dot_general(
+        section_opacity, soot_flat, (((0,), (0,)), ((), ())), preferred_element_type=jnp.float32
     )
+    parts = lax.all_gather(value, "gas", axis=0, tiled=False)
+    summed_all = parts.sum(axis=0)
     own_soot = lax.dynamic_slice_in_dim(summed_all, first_gas, per_gas, 0)
     own_soot = own_soot.reshape((per_gas,) + absorber_molefraction.shape)
     strength = lax.dynamic_slice_in_dim(species_opacity_factor, first_gas, per_gas, 0)

time: 325 us -> 821 us (2.53)
  waiting for transfers between devices: 238 us -> 720 us
  other arithmetic: 11.4 us -> 25.4 us
    all_gather x0 -> x1, waiting for transfers between devices: none -> 640 us  [per_device(): parts = lax.all_gather(value, 'gas', axis=0, tiled=False)]
    psum x1 -> x0, waiting for transfers between devices: 158 us -> none  [per_device(): lax.psum(lax.dot_general(section_opacity, soot_flat, (((0,), (0,)), ((),...]
    reduce_sum x0 -> x1, other arithmetic: none -> 14.1 us  [per_device(): summed_all = parts.sum(axis=0)]
where the time goes in v1:
time: 821 us
  waiting for transfers between devices  720 us (88%)
  starting transfers between devices  29.9 us (4%)
  other arithmetic  25.4 us (3%)
  matrix products  16.8 us (2%)
  between operations  16.2 us (2%)
    all_gather x1, waiting for transfers between devices, per_device(): parts = lax.all_gather(value, 'gas', axis=0, tiled=False)  640 us
    psum x1, waiting for transfers between devices, per_device(): divergence = lax.psum(jnp.sum(gas_terms, axis=0), 'gas')  71.4 us
    ppermute x6, starting transfers between devices, with_halo(): before = lax.ppermute(last, axis, up)  21.9 us
    dot_general x1, matrix products, per_device(): lax.dot_general(section_opacity, soot_flat, (((0,), (0,)), ((), ())), pre...  16.8 us
  transfers between devices with their start and end apart: 14, of which 7 were waited for; matrix products, arithmetic and copies ran while one was open for 0% of the time, Pallas kernels for 0%

profile of v1, /device:TPU:0, one launch (start us, length us, event | category | flops | bytes accessed | tf_op | source)
XLA Modules:
  0.0 820.8 jit_solution(6161626468525109135)
XLA Ops:
  7.9 16.8 %fusion = f32[16,65536]{1,0:T(8,128)} fusion(bf16[128,16]{0,1:T(8,128)(2,1)S(1)} %copy-done, bf16[16,8,512,128]{3,2,1,0:T(8,128)(2,1)} %bitcast.33), kind=kOutput, calls=%fused_computation | convolution fusion | flops 268435456 | bytes 20975616 | tf_op jit(solution)/shard_map/dot_general | solution.py:61
  25.8 639.5 %all-gather.3.cloned.1.call-done = f32[128,65536]{1,0:T(8,128)} async-done(((f32[16,65536]{1,0:T(8,128)}), f32[128,65536]{1,0:T(8,128)}) %all-gather.3.cloned.1.call-update) | async-done | bytes 33554448 | tf_op jit(solution)/shard_map/all_gather | solution.py:64
  665.3 14.1 %reduce_sum.27 = f32[16,65536]{1,0:T(8,128)} reduce(f32[8,16,65536]{2,1,0:T(8,128)} %bitcast.32, f32[]{:T(128)} %constant.8.clone.1), dimensions={0}, to_apply=%region_0.0 | reduce | flops 7340032 | bytes 37748740 | tf_op jit(solution)/shard_map/reduce_sum | solution.py:65
  679.3 1.8 dynamic-slice_bitcast_fusion
  681.9 1.7 collective-permute-start
  683.6 1.3 collective-permute-start.1
  684.9 4.3 collective-permute-start.2
  689.2 1.5 collective-permute-start.3
  691.2 2.4 collective-permute-done.3
  693.5 1.6 add_multiply_fusion.3
  695.2 4.3 collective-permute-start.4
  701.0 1.6 collective-permute-done.5
  703.3 3.8 collective-permute-start.6
  708.6 1.6 collective-permute-done.7
  711.3 3.8 collective-permute-start.8
  716.7 1.6 collective-permute-done.9
  718.3 2.1 add_multiply_fusion
  720.4 3.8 collective-permute-start.10
  725.8 1.6 collective-permute-done.11
  727.4 3.9 fusion.77
  731.2 71.4 %all-reduce.26.cloned.1.call-done = f32[64,8,128]{2,1,0:T(8,128)} async-done(((f32[64,8,128]{2,1,0:T(8,128)}), f32[64,8,128]{2,1,0:T(8,128)}) %all-reduce.26.cloned.1.call-update) | async-done | bytes 262160 | tf_op jit(solution)/shard_map/psum | solution.py:132
  802.6 1.6 reduce_sum.29
  804.2 6.3 psum.15
  811.2 1.7 copy.25
  (59 shorter events, 10.8 us)
Async XLA Ops:
  7.2 0.7 copy-start
  7.2 658.1 %all-gather.3.cloned.1.call-start = ((), (), s32[]{:S(2)}) async-start(), calls=%async_computation.1 | async-start | bytes 37748736 | tf_op jit(solution)/shard_map/all_gather | solution.py:64
  24.7 0.7 copy-start.6
  24.7 0.7 copy-start.5
  24.7 1.0 copy-start.4
  24.7 1.1 copy-start.2
  24.7 777.9 %all-reduce.26.cloned.1.call-start = ((), (), s32[]{:S(2)}) async-start(), calls=%async_computation | async-start | bytes 524288 | tf_op jit(solution)/shard_map/psum | solution.py:132
  665.3 15.8 %copy-start.3 = (f32[64,8,128]{2,1,0:T(8,128)S(1)}, f32[64,8,128]{2,1,0:T(8,128)}, u32[]{:S(2)}) copy-start(f32[64,8,128]{2,1,0:T(8,128)} %param.10) | copy-start | bytes 786436
  681.9 8.8 %collective-permute-start = (f32[2,2,1,8,128]{4,3,2,1,0:T(8,128)S(1)}, f32[2,2,1,8,128]{4,3,2,1,0:T(8,128)S(1)}, u32[]{:S(2)}, u32[]{:S(2)}) collective-permute-start(f32[2,2,1,8,128]{4,3,2,1,0:T(8,128)S(1)} %get-tuple-element.17), channel_id=1, source_target_pairs={{0,1},{1,2},{2,3},{4,5},{5,6},{6,7},{8,9},{9,10},{10,11},{12,13},{... | collective-permute-start | bytes 49160 | tf_op jit(solution)/shard_map/ppermute | solution.py:20
  683.6 7.1 collective-permute-start.1
  684.9 6.2 collective-permute-start.2
  689.2 4.3 collective-permute-start.3
  695.2 5.8 collective-permute-start.4
  699.5 3.1 collective-permute-start.5
  703.3 5.4 collective-permute-start.6
  707.1 3.1 collective-permute-start.7
  711.3 5.4 collective-permute-start.8
  715.2 3.1 collective-permute-start.9
  720.4 5.4 collective-permute-start.10
  724.3 3.1 collective-permute-start.11
  727.4 85.5 %copy-start.1 = (bf16[128,16]{0,1:T(8,128)(2,1)S(1)}, bf16[128,16]{0,1:T(8,128)(2,1)}, u32[]{:S(2)}) copy-start(bf16[128,16]{0,1:T(8,128)(2,1)} %param.8) | copy-start | bytes 12292
Sparse Core Ops, SparseCore 0:
  24.8 640.4 all-gather.2
  731.4 71.2 all-reduce.25
